TPU v7x, 32 devices: a whole 2x2x4 slice. The times are simulated.
32 devices in a mesh: grp: 2 (over x), sec: 16 (over z, y, core).
Axes of the slice: x: 2, y: 2, z: 4, core: 2. Of those that a mesh axis runs over, the one named last changes fastest.
Arguments:
- psi_init: float32 [32, 64, 128], P(('grp', 'sec')), parts along dimension 0, may hold values from -6 to 6
- precond: float32 [32, 64, 128], P(('grp', 'sec')), parts along dimension 0, may hold values from 0.05 to 0.8
- left_ops: bfloat16 [1024, 64, 64], P(('grp', 'sec')), parts along dimension 0, may hold values from -0.75 to 0.75
- right_ops: bfloat16 [1024, 128, 128], P(('grp', 'sec')), parts along dimension 0, may hold values from -0.0234375 to 0.0234375
- term_src: int32 [16384], P(('grp', 'sec')), parts along dimension 0, may hold values from 0 to 15
- term_tgt: int32 [16384], P(('grp', 'sec')), parts along dimension 0, may hold values from 0 to 15
- term_grp: int32 [16384], P(('grp', 'sec')), parts along dimension 0, may hold values from 0 to 31
Outputs:
- psi_final: float32 [32, 64, 128], P(('grp', 'sec')), parts along dimension 0
- sigma_final: float32 [32, 64, 128], P(('grp', 'sec')), parts along dimension 0
- rhos: float32 [6], P('grp'), parts along dimension 0
There are 2 independent parts, one for each index of `grp`. A program takes and returns all parts, laid end to end along the dimension named above; each array names one. Nothing has to cross between parts.
Inputs may be any that keep to these rules, and one draw needn't show every extreme that they name: `term_src`: sector indices. `term_tgt`: sector indices. `term_grp`: local group indices.
All inputs are finite; a program needn't handle non-finite values.
Results may differ from a plain program's by a relative error of at most 0.0045.
Values may be sent and summed in bfloat16 or wider, within the bound.
A program may use at most 128 MiB of HBM per device.

v0:
```python
import jax
import jax.numpy as jnp
from jax import lax
from jax.sharding import PartitionSpec as P

ITERS = 3


def term_parts(trial_all, left_ops, right_ops, term_src, term_grp):
    count = term_src.shape[0]
    width = min(128, count)
    steps_total = count // width
    src_blocks = term_src.reshape(steps_total, width)
    grp_blocks = term_grp.reshape(steps_total, width)

    def one_block(carry, pair):
        sources, groups = pair
        half = jnp.einsum(
            "kab,kbc->kac", left_ops[groups], trial_all[sources], preferred_element_type=jnp.float32
        ).astype(jnp.bfloat16)
        parts = jnp.einsum(
            "kac,kcd->kad", half, right_ops[groups], preferred_element_type=jnp.float32
        )
        return (carry, parts)

    unused, parts = lax.scan(one_block, 0, (src_blocks, grp_blocks))
    return parts.reshape(count, parts.shape[2], parts.shape[3])


def body(psi_init, precond, left_ops, right_ops, term_src, term_tgt, term_grp):
    psi = psi_init
    sectors = psi.shape[0] * lax.axis_size("sec")
    quotients = []
    sigma = psi
    for step in range(ITERS):
        trial_all = lax.all_gather(psi.astype(jnp.bfloat16), "sec", axis=0, tiled=True)
        parts = term_parts(trial_all, left_ops, right_ops, term_src, term_grp)
        partial_sum = (
            jnp.zeros((sectors, psi.shape[1], psi.shape[2]), jnp.float32).at[term_tgt].add(parts)
        )
        sigma = lax.psum_scatter(partial_sum, "sec", scatter_dimension=0, tiled=True)
        self_prod, cross_prod = lax.psum((jnp.sum(psi * psi), jnp.sum(psi * sigma)), "sec")
        rho = cross_prod / self_prod
        fresh = psi - precond * (sigma - rho * psi)
        squared = lax.psum(jnp.sum(fresh * fresh), "sec")
        quotients.append(rho)
        psi = fresh / jnp.sqrt(squared + 1e-06)
    return (psi, sigma, jnp.stack(quotients))


def solution(mesh):
    return jax.shard_map(
        body,
        mesh=mesh,
        in_specs=(
            P(("grp", "sec"), None, None),
            P(("grp", "sec"), None, None),
            P(("grp", "sec"), None, None),
            P(("grp", "sec"), None, None),
            P(("grp", "sec")),
            P(("grp", "sec")),
            P(("grp", "sec")),
        ),
        out_specs=(P(("grp", "sec"), None, None), P(("grp", "sec"), None, None), P("grp")),
        check_vma=False,
    )
```

profile of v0, /device:TPU:0, one launch (start us, length us, event | category | flops | bytes accessed | tf_op | source)
XLA Modules:
  0.0 790.7 jit_solution(5780488434334159570)
XLA Ops:
  8.0 23.8 %all_gather.9 = bf16[16,64,128]{2,1,0:T(8,128)(2,1)S(1)} all-gather(bf16[1,64,128]{2,1,0:T(8,128)(2,1)S(1)} %convert_element_type.18), channel_id=1, replica_groups=mesh['grp'=2,'sec'=16] {'sec'}, dimensions={0}, use_global_device_ids=true | all-gather | bytes 278528 | tf_op jit(solution)/shard_map/all_gather | solution.py:36
  31.8 7.9 broadcast.126.clone.1
  39.7 58.3 %while.30 = (s32[]{:T(128)}, f32[4,128,64,128]{3,2,1,0:T(8,128)}, s32[4,128]{1,0:T(4,128)S(1)}, bf16[32,64,64]{2,1,0:T(8,128)(2,1)S(1)}, s32[4,128]{1,0:T(4,128)...) while((s32[]{:T(128)}, f32[4,128,64,128]{3,2,1,0:T(8,128)}, ...), condition=%wide.region_1.2_spmd, body=%wide.region_0.1_spmd.sunk | while | flops 403704576 | bytes 27276376 | solution.py:26
  39.7 3.0 gather_fusion
  42.7 2.1 gather_fusion.1
  44.9 2.2 gather_fusion.2
  47.0 7.2 bitcast_dynamic-update-slice_fusion.6
  54.2 3.0 gather_fusion
  57.2 2.1 gather_fusion.1
  59.4 2.2 gather_fusion.2
  61.5 7.2 bitcast_dynamic-update-slice_fusion.6
  68.8 3.0 gather_fusion
  71.8 2.1 gather_fusion.1
  74.0 2.2 gather_fusion.2
  76.1 7.3 bitcast_dynamic-update-slice_fusion.6
  83.4 3.0 gather_fusion
  86.4 2.1 gather_fusion.1
  88.5 2.2 gather_fusion.2
  90.7 7.2 bitcast_dynamic-update-slice_fusion.6
  98.0 52.0 %scatter_fusion = f32[16,64,128]{2,1,0:T(8,128)S(1)} fusion(f32[16,64,128]{2,1,0:T(8,128)S(1)} %broadcast.123.clone.1, s32[512]{0:T(512)S(1)} %compare_select_fusion.6, f32[512,64,128]{2,1,0:T(8,128)} %bitcast.107), kind=kCustom, calls=%fused_computation.9 | custom fusion | flops 4194304 | bytes 50333696 | tf_op jit(solution)/shard_map/scatter-add | solution.py:39
  150.9 53.2 %reduce-scatter.4.cloned.1.call-done = f32[1,64,128]{2,1,0:T(8,128)} async-done(((f32[16,64,128]{2,1,0:T(8,128)}), f32[1,64,128]{2,1,0:T(8,128)}) %reduce-scatter.4.cloned.1.call-update) | async-done | bytes 32784 | tf_op jit(solution)/shard_map/reduce_scatter | solution.py:41
  205.5 30.2 %all-reduce.2 = (f32[]{:T(128)}, f32[]{:T(128)}) all-reduce(f32[]{:T(128)} %get-tuple-element.122, f32[]{:T(128)} %get-tuple-element.121), channel_id=1, replica_groups=mesh['grp'=2,'sec'=16] {'sec'}, use_global_device_ids=true, to_apply=%region_5.6 | all-reduce | flops 2 | bytes 16 | tf_op jit(solution)/shard_map/psum | solution.py:42
  238.5 30.1 %psum.65 = f32[]{:T(128)} all-reduce(f32[]{:T(128)} %get-tuple-element.175), channel_id=1, replica_groups=mesh['grp'=2,'sec'=16] {'sec'}, use_global_device_ids=true, to_apply=%region_9.10 | all-reduce | flops 1 | bytes 8 | tf_op jit(solution)/shard_map/psum | solution.py:45
  269.3 17.9 %all_gather.10 = bf16[16,64,128]{2,1,0:T(8,128)(2,1)S(1)} all-gather(bf16[1,64,128]{2,1,0:T(8,128)(2,1)S(1)} %fusion.21), channel_id=1, replica_groups=mesh['grp'=2,'sec'=16] {'sec'}, dimensions={0}, use_global_device_ids=true | all-gather | bytes 278528 | tf_op jit(solution)/shard_map/all_gather | solution.py:36
  287.2 7.9 broadcast.126.clone
  295.1 58.2 %while.31 = (s32[]{:T(128)}, f32[4,128,64,128]{3,2,1,0:T(8,128)}, s32[4,128]{1,0:T(4,128)S(1)}, bf16[32,64,64]{2,1,0:T(8,128)(2,1)S(1)}, s32[4,128]{1,0:T(4,128)...) while((s32[]{:T(128)}, f32[4,128,64,128]{3,2,1,0:T(8,128)}, ...), condition=%wide.region_11.12_spmd, body=%wide.region_10.11_spmd.sunk | while | flops 403704576 | bytes 27276376 | solution.py:26
  295.1 3.0 gather_fusion.3
  298.1 2.1 gather_fusion.4
  300.3 2.2 gather_fusion.5
  302.4 7.2 bitcast_dynamic-update-slice_fusion.7
  309.7 3.0 gather_fusion.3
  312.7 2.1 gather_fusion.4
  314.8 2.2 gather_fusion.5
  317.0 7.2 bitcast_dynamic-update-slice_fusion.7
  324.2 3.0 gather_fusion.3
  327.2 2.1 gather_fusion.4
  329.4 2.2 gather_fusion.5
  331.5 7.3 bitcast_dynamic-update-slice_fusion.7
  338.8 3.0 gather_fusion.3
  344.0 2.2 gather_fusion.5
  346.1 7.2 bitcast_dynamic-update-slice_fusion.7
  353.4 52.0 %scatter_fusion.1 = f32[16,64,128]{2,1,0:T(8,128)S(1)} fusion(f32[16,64,128]{2,1,0:T(8,128)S(1)} %broadcast.123.clone, s32[512]{0:T(512)S(1)} %compare_select_fusion.6, f32[512,64,128]{2,1,0:T(8,128)} %bitcast.108), kind=kCustom, calls=%fused_computation.10 | custom fusion | flops 4194304 | bytes 50333696 | tf_op jit(solution)/shard_map/scatter-add | solution.py:39
  406.3 54.6 %reduce-scatter.6.cloned.1.call-done = f32[1,64,128]{2,1,0:T(8,128)} async-done(((f32[16,64,128]{2,1,0:T(8,128)}), f32[1,64,128]{2,1,0:T(8,128)}) %reduce-scatter.6.cloned.1.call-update) | async-done | bytes 32784 | tf_op jit(solution)/shard_map/reduce_scatter | solution.py:41
  462.2 30.3 %all-reduce.1 = (f32[]{:T(128)}, f32[]{:T(128)}) all-reduce(f32[]{:T(128)} %get-tuple-element.120, f32[]{:T(128)} %get-tuple-element.119), channel_id=1, replica_groups=mesh['grp'=2,'sec'=16] {'sec'}, use_global_device_ids=true, to_apply=%region_15.16 | all-reduce | flops 2 | bytes 16 | tf_op jit(solution)/shard_map/psum | solution.py:42
  495.3 30.1 %psum.68 = f32[]{:T(128)} all-reduce(f32[]{:T(128)} %get-tuple-element.173), channel_id=1, replica_groups=mesh['grp'=2,'sec'=16] {'sec'}, use_global_device_ids=true, to_apply=%region_19.20 | all-reduce | flops 1 | bytes 8 | tf_op jit(solution)/shard_map/psum | solution.py:45
  526.1 18.1 %all_gather.11 = bf16[16,64,128]{2,1,0:T(8,128)(2,1)S(1)} all-gather(bf16[1,64,128]{2,1,0:T(8,128)(2,1)S(1)} %fusion.22), channel_id=1, replica_groups=mesh['grp'=2,'sec'=16] {'sec'}, dimensions={0}, use_global_device_ids=true | all-gather | bytes 278528 | tf_op jit(solution)/shard_map/all_gather | solution.py:36
  544.2 7.9 broadcast.126
  552.1 58.2 %while.32 = (s32[]{:T(128)}, f32[4,128,64,128]{3,2,1,0:T(8,128)}, s32[4,128]{1,0:T(4,128)S(1)}, bf16[32,64,64]{2,1,0:T(8,128)(2,1)S(1)}, s32[4,128]{1,0:T(4,128)...) while((s32[]{:T(128)}, f32[4,128,64,128]{3,2,1,0:T(8,128)}, ...), condition=%wide.region_21.22_spmd, body=%wide.region_20.21_spmd.sunk | while | flops 403704576 | bytes 27276376 | solution.py:26
  552.1 3.0 gather_fusion.6
  557.2 2.2 gather_fusion.8
  559.4 7.2 bitcast_dynamic-update-slice_fusion.8
  566.6 3.0 gather_fusion.6
  571.8 2.2 gather_fusion.8
  573.9 7.2 bitcast_dynamic-update-slice_fusion.8
  581.2 3.0 gather_fusion.6
  586.3 2.2 gather_fusion.8
  588.5 7.3 bitcast_dynamic-update-slice_fusion.8
  595.8 3.0 gather_fusion.6
  600.9 2.2 gather_fusion.8
  603.1 7.2 bitcast_dynamic-update-slice_fusion.8
  610.4 52.0 %scatter_fusion.2 = f32[16,64,128]{2,1,0:T(8,128)S(1)} fusion(f32[16,64,128]{2,1,0:T(8,128)S(1)} %broadcast.123, s32[512]{0:T(512)S(1)} %compare_select_fusion.6, f32[512,64,128]{2,1,0:T(8,128)} %bitcast.109), kind=kCustom, calls=%fused_computation.11 | custom fusion | flops 4194304 | bytes 50333696 | tf_op jit(solution)/shard_map/scatter-add | solution.py:39
  663.2 54.6 %reduce-scatter.8.cloned.1.call-done = f32[1,64,128]{2,1,0:T(8,128)} async-done(((f32[16,64,128]{2,1,0:T(8,128)}), f32[1,64,128]{2,1,0:T(8,128)}) %reduce-scatter.8.cloned.1.call-update) | async-done | bytes 32784 | tf_op jit(solution)/shard_map/reduce_scatter | solution.py:41
  719.2 30.2 %all-reduce = (f32[]{:T(128)}, f32[]{:T(128)}) all-reduce(f32[]{:T(128)} %get-tuple-element.118, f32[]{:T(128)} %get-tuple-element.117), channel_id=1, replica_groups=mesh['grp'=2,'sec'=16] {'sec'}, use_global_device_ids=true, to_apply=%region_25.26 | all-reduce | flops 2 | bytes 16 | tf_op jit(solution)/shard_map/psum | solution.py:42
  752.2 30.1 %psum.71 = f32[]{:T(128)} all-reduce(f32[]{:T(128)} %get-tuple-element.171), channel_id=1, replica_groups=mesh['grp'=2,'sec'=16] {'sec'}, use_global_device_ids=true, to_apply=%region_29.30 | all-reduce | flops 1 | bytes 8 | tf_op jit(solution)/shard_map/psum | solution.py:45
  (82 shorter events, 23.9 us)
Async XLA Ops:
  7.2 196.9 %reduce-scatter.4.cloned.1.call-start = ((), (), s32[]{:S(2)}) async-start(), calls=%async_computation.3 | async-start | bytes 557056 | tf_op jit(solution)/shard_map/reduce_scatter | solution.py:41
  31.8 7.9 copy-start
  31.8 7.9 copy-start.1
  31.8 7.9 copy-start.7
  31.8 7.9 copy-start.8
  39.6 58.3 %copy-start.9 = (s32[512]{0:T(512)S(1)}, s32[512]{0:T(512)}, u32[]{:S(2)}) copy-start(s32[512]{0:T(512)} %param.18) | copy-start | bytes 6148
  98.0 106.1 %copy-start.5 = (f32[1,64,128]{2,1,0:T(8,128)S(1)}, f32[1,64,128]{2,1,0:T(8,128)}, u32[]{:S(2)}) copy-start(f32[1,64,128]{2,1,0:T(8,128)} %param.13) | copy-start | bytes 98308
  98.0 139.1 %copy-start.6 = (f32[1,64,128]{2,1,0:T(8,128)S(1)}, f32[1,64,128]{2,1,0:T(8,128)}, u32[]{:S(2)}) copy-start(f32[1,64,128]{2,1,0:T(8,128)} %param.14) | copy-start | bytes 98308
  150.1 0.8 copy-start.3
  150.9 310.0 %reduce-scatter.6.cloned.1.call-start = ((), (), s32[]{:S(2)}) async-start(), calls=%async_computation.4 | async-start | bytes 557056 | tf_op jit(solution)/shard_map/reduce_scatter | solution.py:41
  405.5 0.8 copy-start.4
  406.3 311.6 %reduce-scatter.8.cloned.1.call-start = ((), (), s32[]{:S(2)}) async-start(), calls=%async_computation.5 | async-start | bytes 557056 | tf_op jit(solution)/shard_map/reduce_scatter | solution.py:41
  662.4 0.8 copy-start.2
Sparse Core Ops, SparseCore 0:
  151.0 53.0 reduce-scatter.3
  406.4 54.4 reduce-scatter.5
  663.3 54.4 reduce-scatter.7
where the time goes:
time: 796 us; the launch traced here: 791 us
  blocking collectives  241 us (30%)
  other arithmetic  167 us (21%)
  waiting for transfers between devices  162 us (20%)
  local copies, waits for them, and re-layouts  114 us (14%)
  matrix products  86.8 us (11%)
  between operations  20 us (3%)
    reduce_scatter x3, waiting for transfers between devices, body(): lax.psum_scatter(partial_sum, 'sec', scatter_dimension=0, tiled=True)  162 us
    scatter-add x3, other arithmetic, body(): jnp.zeros((sectors, psi.shape[1], psi.shape[2]), jnp.float32).at[term_tgt]  156 us
    psum x3, blocking collectives, body(): lax.psum((jnp.sum(psi * psi), jnp.sum(psi * sigma)), 'sec')  90.8 us
    psum x3, blocking collectives, body(): squared = lax.psum(jnp.sum(fresh * fresh), 'sec')  90.3 us
    dot_general x12, matrix products, one_block(): jnp.einsum('kac,kcd->kad', half, right_ops[groups], preferred_element_typ...  86.8 us
    all_gather x3, blocking collectives, body(): lax.all_gather(psi.astype(jnp.bfloat16), 'sec', axis=0, tiled=True)  59.9 us
    gather x12, local copies, waits for them, and re-layouts, one_block(): right_ops[groups]  36.1 us
    gather x12, local copies, waits for them, and re-layouts, one_block(): trial_all[sources]  25.9 us
  transfers between devices with their start and end apart: 3, of which 3 were waited for; matrix products, arithmetic and copies ran while one was open for 0% of the time, Pallas kernels for 0%

commit v1 on v0

v1 whole, which is shorter than its diff:
```python
import functools

import jax
import jax.numpy as jnp
from jax import lax
from jax.experimental import pallas as pl
from jax.experimental.pallas import tpu as pltpu
from jax.sharding import PartitionSpec as P

ITERS = 3
F32 = jnp.float32
BF16 = jnp.bfloat16
MESH = pl.DeviceIdType.MESH


def kernel(
    n, count, groups, bl, br, chunk,
    term_ref, psi_ref, pre_ref, left_ref, right_ref,
    psi_out, sig_out, rho_out,
    psi_recv, pre_recv, u_recv, s_recv, sib_send, sib_recv, sig_send, sig_recv, full_send, full_recv,
    own, all_psi, plan_buf, keep_buf, place_buf, src_ref, keep_ref, place_ref, plan_sem, seg, left2, a_buf, send_sem, recv_sem,
):
    me = lax.axis_index("sec")
    chips = n // 2
    core = lax.rem(me, 2)
    chip = me // 2
    sibling = me + 1 - 2 * core
    PSI, PRE, SIB, SIG, SCAL, UPD = 0, 1, 2, 2 + ITERS, 2 + 2 * ITERS, 2 + 3 * ITERS

    def push(stage, source, target, peer):
        pltpu.make_async_remote_copy(
            src_ref=source,
            dst_ref=target,
            send_sem=send_sem.at[stage],
            recv_sem=recv_sem.at[stage],
            device_id={"sec": peer},
            device_id_type=MESH,
        ).start()

    def push_all(stage, ref):
        def one(d, _):
            push(stage, ref.at[me], ref.at[me], lax.rem(me + d, n))
            return 0

        lax.fori_loop(1, n, one, 0)

    def wait_for(sem, stage, span):
        pltpu.make_async_copy(span, span, sem.at[stage]).wait()

    others = pl.ds(0, n - 1)
    other_chips = pl.ds(0, chips - 1)

    barrier = pltpu.get_barrier_semaphore()

    def greet(d, _):
        pl.semaphore_signal(barrier, inc=1, device_id={"sec": lax.rem(me + d, n)}, device_id_type=MESH)
        return 0

    lax.fori_loop(1, n, greet, 0)
    psi_recv[me] = psi_ref[0].astype(BF16)
    pre_recv[me] = pre_ref[0].astype(BF16)
    pl.semaphore_wait(barrier, n - 1)
    push_all(PSI, psi_recv)
    push_all(PRE, pre_recv)

    psi_out[0] = psi_ref[0]
    seg[count] = jnp.zeros((2 * bl, br), BF16)

    def double(g, _):
        left2[g] = jnp.concatenate([left_ref[g], left_ref[g]], axis=1)
        return 0

    lax.fori_loop(0, groups, double, 0)
    sort_terms(term_ref, plan_buf, keep_buf, place_buf, n, count, groups)
    moves = [
        pltpu.make_async_copy(a, b, plan_sem.at[i])
        for i, (a, b) in enumerate([(plan_buf, src_ref), (keep_buf, keep_ref), (place_buf, place_ref)])
    ]
    for move in moves:
        move.start()
    for move in moves:
        move.wait()
    wait_for(recv_sem, PSI, psi_recv.at[others])

    def unpack(s, _):
        all_psi[s] = psi_recv[s].astype(F32)
        return 0

    lax.fori_loop(0, n, unpack, 0)

    def apply(parity, store, split):
        depth = 2 * bl if split else bl
        lefts = left2 if split else left_ref

        def some(c, _):
            def one_group(g, _):
                first = g * n + c * (2 * chunk) + parity
                blocks = [seg[jnp.clip(place_ref[0, first + 2 * t], 0, count), :depth, :] for t in range(chunk)]
                half = jnp.dot(lefts[g], jnp.concatenate(blocks, axis=1), preferred_element_type=F32)
                half = half.astype(BF16)
                lanes = pl.ds(pl.multiple_of(g * br, br), br)
                for t in range(chunk):
                    a_buf[t * bl:(t + 1) * bl, lanes] = half[:, t * br:(t + 1) * br]
                return 0

            lax.fori_loop(0, groups, one_group, 0, unroll=8)
            store(c, jnp.dot(a_buf[...], right_ref[...], preferred_element_type=F32).reshape(chunk, bl, br))
            return 0

        lax.fori_loop(0, chips // chunk, some, 0)

    unroll = 8
    for step in range(ITERS):
        last = step == ITERS - 1

        def mix(block, acc):
            for j in range(unroll):
                k = block * unroll + j
                acc = acc * keep_ref[0, k] + all_psi[jnp.clip(src_ref[0, k], 0, n - 1)]
                high = acc.astype(BF16)
                seg[k, :bl, :] = high
                if last:
                    seg[k, bl:, :] = (acc - high.astype(F32)).astype(BF16)
            return acc

        lax.fori_loop(0, count // unroll, mix, jnp.zeros((bl, br), F32))

        def to_sibling(c, value):
            sib_send[pl.ds(c * chunk, chunk)] = value

        def to_owner(c, value):
            own[pl.ds(c * chunk, chunk)] = value

        if step > 0:
            wait_for(send_sem, SIB + step - 1, sib_send)
        apply(1 - core, to_sibling, last)
        push(SIB + step, sib_send, sib_recv.at[step], sibling)
        apply(core, to_owner, last)
        wait_for(recv_sem, SIB + step, sib_recv.at[step])

        if last:
            leaving, arriving = full_send, full_recv
        else:
            leaving, arriving = sig_send, sig_recv.at[step]
        if 0 < step < ITERS - 1:
            wait_for(send_sem, SIG + step - 1, sig_send.at[other_chips])

        def forward(d, _):
            to = lax.rem(chip + d, chips)
            leaving[to] = (own[to] + sib_recv[step, to]).astype(leaving.dtype)
            push(SIG + step, leaving.at[to], arriving.at[chip], 2 * to + core)
            return 0

        lax.fori_loop(1, chips, forward, 0)
        mine = own[chip] + sib_recv[step, chip]
        arriving[chip] = jnp.zeros((bl, br), arriving.dtype)
        wait_for(recv_sem, SIG + step, arriving.at[other_chips])
        sigma = lax.fori_loop(0, chips, lambda c, acc: acc + arriving[c].astype(F32), mine)

        psi = psi_out[0]
        pre = pre_ref[0]
        u = psi - pre * sigma
        v = pre * psi
        rows = [jnp.sum(x, axis=0, keepdims=True) for x in (psi * psi, psi * sigma, u * u, u * v, v * v)]
        s_recv[step, me] = jnp.concatenate(rows + [jnp.zeros((3, br), F32)], axis=0)
        push_all(SCAL + step, s_recv.at[step])
        if last:
            sig_out[0] = sigma
        else:
            u_recv[step, me] = u.astype(BF16)
            push_all(UPD + step, u_recv.at[step])
        wait_for(recv_sem, SCAL + step, s_recv.at[step, others])
        total = jnp.sum(jnp.sum(s_recv[step], axis=0), axis=1, keepdims=True)
        rho = total[1:2] / total[0:1]
        norm = total[2:3] + 2.0 * rho * total[3:4] + rho * rho * total[4:5]
        inv = 1.0 / jnp.sqrt(norm + 1e-06)
        rho_out[step:step + 1, :] = jnp.broadcast_to(rho, (1, br))
        psi_out[0] = (u + rho * v) * inv
        if not last:
            if step == 0:
                wait_for(recv_sem, PRE, pre_recv.at[others])
            wait_for(recv_sem, UPD + step, u_recv.at[step, others])

            def update(s, _):
                pre_s = pre_recv[s].astype(F32)
                all_psi[s] = (u_recv[step, s].astype(F32) + rho * (pre_s * all_psi[s])) * inv
                return 0

            lax.fori_loop(0, n, update, 0)

    rho_out[ITERS:, :] = jnp.zeros((8 - ITERS, br), F32)
    wait_for(send_sem, PSI, psi_recv.at[others])
    wait_for(send_sem, PRE, pre_recv.at[others])
    wait_for(send_sem, SIB + ITERS - 1, sib_send)
    wait_for(send_sem, SIG + ITERS - 2, sig_send.at[other_chips])
    wait_for(send_sem, SIG + ITERS - 1, full_send.at[other_chips])
    for step in range(ITERS):
        wait_for(send_sem, SCAL + step, s_recv.at[step, others])
        if step < ITERS - 1:
            wait_for(send_sem, UPD + step, u_recv.at[step, others])


def sort_terms(term_ref, src_buf, keep_buf, place_buf, n, count, groups):
    I32 = jnp.int32
    key = term_ref[2:3, :] * n + term_ref[1:2, :]
    rows = jnp.concatenate([key, term_ref[0:1, :], key, key, key, key, key, key], axis=0)
    columns = jnp.transpose(rows)
    key_col, src_col = columns[:, 0:1], columns[:, 1:2]
    at = lax.broadcasted_iota(I32, (1, count), 1)
    code = key * count + at
    code_col = key_col * count + lax.broadcasted_iota(I32, (count, 1), 0)

    def tally(which):
        return jnp.sum(jnp.where(which, 1, 0), axis=0, keepdims=True)

    rank = jnp.transpose(jnp.broadcast_to(tally(code_col < code), (8, count)))[:, 0:1]
    here = rank == at
    sources = jnp.sum(jnp.where(here, src_col, 0), axis=0, keepdims=True)
    src_buf[...] = jnp.clip(sources, 0, n - 1)
    ordered = jnp.sum(jnp.where(here, key_col + 1, 0), axis=0, keepdims=True)
    before = jnp.sum(jnp.where(rank + 1 == at, key_col + 1, 0), axis=0, keepdims=True)
    keep_buf[...] = jnp.where(ordered == before, 1.0, 0.0)
    for c in range(groups * n // count):
        pair = at + c * count
        upto = tally(key_col <= pair)
        place = jnp.where(upto > tally(key_col < pair), upto - 1, count)
        place_buf[:, c * count:(c + 1) * count] = jnp.clip(place, 0, count)


def body(n, psi_init, precond, left_ops, right_ops, term_src, term_tgt, term_grp):
    local, bl, br = psi_init.shape
    assert local == 1
    groups = left_ops.shape[0]
    count = term_src.shape[0]
    chunk = min(n // 2, 8)
    terms = jnp.stack([term_src, term_tgt, term_grp])
    assert groups * n % count == 0
    rights = right_ops.reshape(groups * br, br)
    vmem = pl.BlockSpec(memory_space=pltpu.VMEM)
    stages = 2 + 4 * ITERS
    psi, sigma, rhos = pl.pallas_call(
        functools.partial(kernel, n, count, groups, bl, br, chunk),
        out_shape=(
            jax.ShapeDtypeStruct((1, bl, br), F32),
            jax.ShapeDtypeStruct((1, bl, br), F32),
            jax.ShapeDtypeStruct((8, br), F32),
        ),
        in_specs=[vmem] * 5,
        out_specs=(vmem, vmem, vmem),
        scratch_shapes=[
            pltpu.VMEM((n, bl, br), BF16),
            pltpu.VMEM((n, bl, br), BF16),
            pltpu.VMEM((ITERS - 1, n, bl, br), BF16),
            pltpu.VMEM((ITERS, n, 8, br), F32),
            pltpu.VMEM((n // 2, bl, br), F32),
            pltpu.VMEM((ITERS, n // 2, bl, br), F32),
            pltpu.VMEM((n // 2, bl, br), BF16),
            pltpu.VMEM((ITERS - 1, n // 2, bl, br), BF16),
            pltpu.VMEM((n // 2, bl, br), F32),
            pltpu.VMEM((n // 2, bl, br), F32),
            pltpu.VMEM((n // 2, bl, br), F32),
            pltpu.VMEM((n, bl, br), F32),
            pltpu.VMEM((1, count), jnp.int32),
            pltpu.VMEM((1, count), F32),
            pltpu.VMEM((1, groups * n), jnp.int32),
            pltpu.SMEM((1, count), jnp.int32),
            pltpu.SMEM((1, count), F32),
            pltpu.SMEM((1, groups * n), jnp.int32),
            pltpu.SemaphoreType.DMA((3,)),
            pltpu.VMEM((count + 1, 2 * bl, br), BF16),
            pltpu.VMEM((groups, bl, 2 * bl), BF16),
            pltpu.VMEM((chunk * bl, groups * br), BF16),
            pltpu.SemaphoreType.DMA((stages,)),
            pltpu.SemaphoreType.DMA((stages,)),
        ],
        compiler_params=pltpu.CompilerParams(
            collective_id=0, has_side_effects=True, vmem_limit_bytes=56 * 1024 * 1024
        ),
    )(terms, psi_init, precond, left_ops, rights)
    return psi, sigma, rhos[:ITERS, 0]


def solution(mesh):
    return jax.shard_map(
        functools.partial(body, mesh.shape["sec"]),
        mesh=mesh,
        in_specs=(
            P(("grp", "sec"), None, None),
            P(("grp", "sec"), None, None),
            P(("grp", "sec"), None, None),
            P(("grp", "sec"), None, None),
            P(("grp", "sec")),
            P(("grp", "sec")),
            P(("grp", "sec")),
        ),
        out_specs=(P(("grp", "sec"), None, None), P(("grp", "sec"), None, None), P("grp")),
        check_vma=False,
    )
```

time: 796 us -> 88.5 us (0.11)
  blocking collectives: 241 us -> 0 us
  other arithmetic: 167 us -> 0.61 us
  waiting for transfers between devices: 162 us -> 0 us
  local copies, waits for them, and re-layouts: 114 us -> 3.98 us
  matrix products: 86.8 us -> 0 us
  Pallas kernels: 0 us -> 83 us
  between operations: 20 us -> 0.68 us
    psum x6 -> x0, blocking collectives: 181 us -> none  [the longest x3 90.8 us: body(): lax.psum((jnp.sum(psi * psi), jnp.sum(psi * sigma)), 'sec')]
    reduce_scatter x3 -> x0, waiting for transfers between devices: 162 us -> none  [body(): lax.psum_scatter(partial_sum, 'sec', scatter_dimension=0, tiled=True)]
    scatter-add x3 -> x0, other arithmetic: 156 us -> none  [body(): jnp.zeros((sectors, psi.shape[1], psi.shape[2]), jnp.float32).at[term_tgt]]
    gather x36 -> x0, local copies, waits for them, and re-layouts: 87.6 us -> none  [the longest x12 36.1 us: one_block(): right_ops[groups]]
    dot_general x12 -> x0, matrix products: 86.8 us -> none  [one_block(): jnp.einsum('kac,kcd->kad', half, right_ops[groups], preferred_element_typ...]
    pallas_call x0 -> x1, Pallas kernels: none -> 83 us  [body(): pl.pallas_call(functools.partial(kernel, n, count, groups, bl, br, chunk)...]
    all_gather x3 -> x0, blocking collectives: 59.9 us -> none  [body(): lax.all_gather(psi.astype(jnp.bfloat16), 'sec', axis=0, tiled=True)]
    another operation x6 -> x0, local copies, waits for them, and re-layouts: 23.7 us -> none
  transfers between devices with their start and end apart: 3 -> 0, of which waited for: 3 -> 0; matrix products, arithmetic and copies ran while one was open for 0% -> 0% of each run, Pallas kernels for 0% -> 0%
where the time goes in v1:
time: 88.5 us; the launch traced here: 88.3 us
  Pallas kernels  83 us (94%)
  local copies, waits for them, and re-layouts  3.98 us (4%)
    pallas_call x1, Pallas kernels, body(): pl.pallas_call(functools.partial(kernel, n, count, groups, bl, br, chunk)...  83 us
    unnamed x12, local copies, waits for them, and re-layouts  3.35 us

profile of v1, /device:TPU:0, one launch (start us, length us, event | category | flops | bytes accessed | tf_op | source)
XLA Modules:
  0.0 88.3 jit_solution(14384883357357321913)
XLA Ops:
  0.6 0.0 copy-start.3
  0.6 0.0 copy-start.2
  0.7 0.0 copy-start.1
  0.7 0.7 copy-done.3
  1.3 0.0 copy-done.2
  1.3 0.0 copy-done.1
  1.3 0.6 pad_add_fusion.term_ref
  2.0 83.0 %shard_map.94 = (f32[1,64,128]{2,1,0:T(8,128)}, f32[1,64,128]{2,1,0:T(8,128)}, f32[8,128]{1,0:T(8,128)}) custom-call(s32[3,512]{1,0:T(4,128)} %pad_add_fusion.term_ref, f32[1,64,128]{2,1,0:T(8,128)} %psi_ref.1, f32[1,64,128]{2,1,0:T(8,128)} %pre_ref.1, bf16[32,64,64]{2,1,0:T(8,128)(2,1)} %left_ref.1, bf16[4096,128]{1,0:T(8,128)(2,1)} %bitcast.4), custom_call_target="tpu_custom_call" | custom-call | tf_op jit(solution)/shard_map/pallas_call | solution.py:241
  85.0 0.0 copy-start.4
  85.0 0.7 copy-done.4
  85.7 0.6 slice_reduce_fusion
  86.3 0.0 copy-start
  86.3 1.4 %copy.12 = f32[1,64,128]{2,1,0:T(8,128)} copy(f32[1,64,128]{2,1,0:T(8,128)} %get-tuple-element.12) | data formatting | bytes 65536
  87.7 0.0 copy-done
  87.7 0.6 copy.13
Async XLA Ops:
  0.6 0.7 copy-start.3
  0.6 0.7 copy-start.2
  0.7 0.7 copy-start.1
  85.0 0.7 copy-start.4
  86.3 1.4 %copy-start = (f32[1,64,128]{2,1,0:T(8,128)S(1)}, f32[1,64,128]{2,1,0:T(8,128)}, u32[]{:S(2)}) copy-start(f32[1,64,128]{2,1,0:T(8,128)} %get-tuple-element.13) | copy-start | bytes 98308

commit v2 on v1

--- a/solution.py
+++ b/solution.py
@@ -14,16 +14,18 @@
 
 
 def kernel(
-    n, count, groups, bl, br, chunk,
-    term_ref, psi_ref, pre_ref, left_ref, right_ref,
+    n, count, groups, bl, br,
+    term_src, term_tgt, term_grp, psi_ref, pre_ref, left_ref, right_ref,
     psi_out, sig_out, rho_out,
     psi_recv, pre_recv, u_recv, s_recv, sib_send, sib_recv, sig_send, sig_recv, full_send, full_recv,
-    own, all_psi, plan_buf, keep_buf, place_buf, src_ref, keep_ref, place_ref, plan_sem, seg, left2, a_buf, send_sem, recv_sem,
+    own, all_psi, plan_buf, keep_buf, place_buf, src_ref, keep_ref, place_ref, plan_sem, seg, left2, a_buf, send_sem, recv_sem, near_sem,
 ):
     me = lax.axis_index("sec")
     chips = n // 2
     core = lax.rem(me, 2)
     chip = me // 2
+    span = chips // 2
+    side = chip // span
     sibling = me + 1 - 2 * core
     PSI, PRE, SIB, SIG, SCAL, UPD = 0, 1, 2, 2 + ITERS, 2 + 2 * ITERS, 2 + 3 * ITERS
 
@@ -47,6 +49,32 @@
     def wait_for(sem, stage, span):
         pltpu.make_async_copy(span, span, sem.at[stage]).wait()
 
+    def gather(stage, row, ref):
+        push(stage, ref.at[me], ref.at[me], sibling)
+
+        def one(d, _):
+            pltpu.make_async_remote_copy(
+                src_ref=ref.at[me],
+                dst_ref=ref.at[me],
+                send_sem=send_sem.at[stage],
+                recv_sem=near_sem.at[row, d],
+                device_id={"sec": 2 * lax.rem(chip + d, chips) + core},
+                device_id_type=MESH,
+            ).start()
+            return 0
+
+        lax.fori_loop(1, chips, one, 0)
+
+    def hand_on(stage, row, ref):
+        def one(d, _):
+            block = ref.at[2 * lax.rem(chip - d + chips, chips) + core]
+            pltpu.make_async_copy(block, block, near_sem.at[row, d]).wait()
+            push(stage, block, block, sibling)
+            return 0
+
+        lax.fori_loop(1, chips, one, 0)
+        wait_for(recv_sem, stage, ref.at[pl.ds(0, chips)])
+
     others = pl.ds(0, n - 1)
     other_chips = pl.ds(0, chips - 1)
 
@@ -60,8 +88,7 @@
     psi_recv[me] = psi_ref[0].astype(BF16)
     pre_recv[me] = pre_ref[0].astype(BF16)
     pl.semaphore_wait(barrier, n - 1)
-    push_all(PSI, psi_recv)
-    push_all(PRE, pre_recv)
+    gather(PSI, 0, psi_recv)
 
     psi_out[0] = psi_ref[0]
     seg[count] = jnp.zeros((2 * bl, br), BF16)
@@ -71,7 +98,7 @@
         return 0
 
     lax.fori_loop(0, groups, double, 0)
-    sort_terms(term_ref, plan_buf, keep_buf, place_buf, n, count, groups)
+    sort_terms(term_src, term_tgt, term_grp, plan_buf, keep_buf, place_buf, n, count, groups)
     moves = [
         pltpu.make_async_copy(a, b, plan_sem.at[i])
         for i, (a, b) in enumerate([(plan_buf, src_ref), (keep_buf, keep_ref), (place_buf, place_ref)])
@@ -80,7 +107,8 @@
         move.start()
     for move in moves:
         move.wait()
-    wait_for(recv_sem, PSI, psi_recv.at[others])
+    hand_on(PSI, 0, psi_recv)
+    push_all(PRE, pre_recv)
 
     def unpack(s, _):
         all_psi[s] = psi_recv[s].astype(F32)
@@ -88,13 +116,15 @@
 
     lax.fori_loop(0, n, unpack, 0)
 
-    def apply(parity, store, split):
+    def apply(parity, start, length, out, split):
+        chunk = min(length, 8)
+        height = chunk * bl
         depth = 2 * bl if split else bl
         lefts = left2 if split else left_ref
 
         def some(c, _):
             def one_group(g, _):
-                first = g * n + c * (2 * chunk) + parity
+                first = g * n + 2 * (start + c * chunk) + parity
                 blocks = [seg[jnp.clip(place_ref[0, first + 2 * t], 0, count), :depth, :] for t in range(chunk)]
                 half = jnp.dot(lefts[g], jnp.concatenate(blocks, axis=1), preferred_element_type=F32)
                 half = half.astype(BF16)
@@ -104,10 +134,11 @@
                 return 0
 
             lax.fori_loop(0, groups, one_group, 0, unroll=8)
-            store(c, jnp.dot(a_buf[...], right_ref[...], preferred_element_type=F32).reshape(chunk, bl, br))
-            return 0
-
-        lax.fori_loop(0, chips // chunk, some, 0)
+            prod = jnp.dot(a_buf[:height, :], right_ref[...], preferred_element_type=F32)
+            out[pl.ds(start + c * chunk, chunk)] = prod.reshape(chunk, bl, br)
+            return 0
+
+        lax.fori_loop(0, length // chunk, some, 0)
 
     unroll = 8
     for step in range(ITERS):
@@ -125,19 +156,10 @@
 
         lax.fori_loop(0, count // unroll, mix, jnp.zeros((bl, br), F32))
 
-        def to_sibling(c, value):
-            sib_send[pl.ds(c * chunk, chunk)] = value
-
-        def to_owner(c, value):
-            own[pl.ds(c * chunk, chunk)] = value
-
         if step > 0:
             wait_for(send_sem, SIB + step - 1, sib_send)
-        apply(1 - core, to_sibling, last)
+        apply(1 - core, 0, chips, sib_send, last)
         push(SIB + step, sib_send, sib_recv.at[step], sibling)
-        apply(core, to_owner, last)
-        wait_for(recv_sem, SIB + step, sib_recv.at[step])
-
         if last:
             leaving, arriving = full_send, full_recv
         else:
@@ -145,13 +167,23 @@
         if 0 < step < ITERS - 1:
             wait_for(send_sem, SIG + step - 1, sig_send.at[other_chips])
 
-        def forward(d, _):
-            to = lax.rem(chip + d, chips)
+        def forward(to):
             leaving[to] = (own[to] + sib_recv[step, to]).astype(leaving.dtype)
             push(SIG + step, leaving.at[to], arriving.at[chip], 2 * to + core)
-            return 0
-
-        lax.fori_loop(1, chips, forward, 0)
+
+        def far(j, _):
+            forward((1 - side) * span + j)
+            return 0
+
+        def near(d, _):
+            forward(side * span + lax.rem(chip - side * span + d, span))
+            return 0
+
+        apply(core, (1 - side) * span, span, own, last)
+        wait_for(recv_sem, SIB + step, sib_recv.at[step])
+        lax.fori_loop(0, span, far, 0)
+        apply(core, side * span, span, own, last)
+        lax.fori_loop(1, span, near, 0)
         mine = own[chip] + sib_recv[step, chip]
         arriving[chip] = jnp.zeros((bl, br), arriving.dtype)
         wait_for(recv_sem, SIG + step, arriving.at[other_chips])
@@ -163,12 +195,14 @@
         v = pre * psi
         rows = [jnp.sum(x, axis=0, keepdims=True) for x in (psi * psi, psi * sigma, u * u, u * v, v * v)]
         s_recv[step, me] = jnp.concatenate(rows + [jnp.zeros((3, br), F32)], axis=0)
-        push_all(SCAL + step, s_recv.at[step])
         if last:
             sig_out[0] = sigma
+            push_all(SCAL + step, s_recv.at[step])
         else:
             u_recv[step, me] = u.astype(BF16)
-            push_all(UPD + step, u_recv.at[step])
+            gather(UPD + step, 1 + step, u_recv.at[step])
+            push_all(SCAL + step, s_recv.at[step])
+            hand_on(UPD + step, 1 + step, u_recv.at[step])
         wait_for(recv_sem, SCAL + step, s_recv.at[step, others])
         total = jnp.sum(jnp.sum(s_recv[step], axis=0), axis=1, keepdims=True)
         rho = total[1:2] / total[0:1]
@@ -179,14 +213,13 @@
         if not last:
             if step == 0:
                 wait_for(recv_sem, PRE, pre_recv.at[others])
-            wait_for(recv_sem, UPD + step, u_recv.at[step, others])
 
             def update(s, _):
                 pre_s = pre_recv[s].astype(F32)
                 all_psi[s] = (u_recv[step, s].astype(F32) + rho * (pre_s * all_psi[s])) * inv
                 return 0
 
-            lax.fori_loop(0, n, update, 0)
+            lax.fori_loop(0, n, update, 0, unroll=4)
 
     rho_out[ITERS:, :] = jnp.zeros((8 - ITERS, br), F32)
     wait_for(send_sem, PSI, psi_recv.at[others])
@@ -200,10 +233,10 @@
             wait_for(send_sem, UPD + step, u_recv.at[step, others])
 
 
-def sort_terms(term_ref, src_buf, keep_buf, place_buf, n, count, groups):
+def sort_terms(term_src, term_tgt, term_grp, src_buf, keep_buf, place_buf, n, count, groups):
     I32 = jnp.int32
-    key = term_ref[2:3, :] * n + term_ref[1:2, :]
-    rows = jnp.concatenate([key, term_ref[0:1, :], key, key, key, key, key, key], axis=0)
+    key = term_grp[...] * n + term_tgt[...]
+    rows = jnp.concatenate([key, term_src[...], key, key, key, key, key, key], axis=0)
     columns = jnp.transpose(rows)
     key_col, src_col = columns[:, 0:1], columns[:, 1:2]
     at = lax.broadcasted_iota(I32, (1, count), 1)
@@ -233,19 +266,18 @@
     groups = left_ops.shape[0]
     count = term_src.shape[0]
     chunk = min(n // 2, 8)
-    terms = jnp.stack([term_src, term_tgt, term_grp])
     assert groups * n % count == 0
     rights = right_ops.reshape(groups * br, br)
     vmem = pl.BlockSpec(memory_space=pltpu.VMEM)
     stages = 2 + 4 * ITERS
     psi, sigma, rhos = pl.pallas_call(
-        functools.partial(kernel, n, count, groups, bl, br, chunk),
+        functools.partial(kernel, n, count, groups, bl, br),
         out_shape=(
             jax.ShapeDtypeStruct((1, bl, br), F32),
             jax.ShapeDtypeStruct((1, bl, br), F32),
             jax.ShapeDtypeStruct((8, br), F32),
         ),
-        in_specs=[vmem] * 5,
+        in_specs=[vmem] * 7,
         out_specs=(vmem, vmem, vmem),
         scratch_shapes=[
             pltpu.VMEM((n, bl, br), BF16),
@@ -272,11 +304,12 @@
             pltpu.VMEM((chunk * bl, groups * br), BF16),
             pltpu.SemaphoreType.DMA((stages,)),
             pltpu.SemaphoreType.DMA((stages,)),
+            pltpu.SemaphoreType.DMA((ITERS, n // 2)),
         ],
         compiler_params=pltpu.CompilerParams(
             collective_id=0, has_side_effects=True, vmem_limit_bytes=56 * 1024 * 1024
         ),
-    )(terms, psi_init, precond, left_ops, rights)
+    )(*[t.reshape(1, count) for t in (term_src, term_tgt, term_grp)], psi_init, precond, left_ops, rights)
     return psi, sigma, rhos[:ITERS, 0]
 
 

time: 88.5 us -> 78.4 us (0.89)
  Pallas kernels: 83 us -> 74.2 us
    pallas_call x1, Pallas kernels: 83 us -> 74.2 us  [body(): pl.pallas_call(functools.partial(kernel, n, count, groups, bl, br), out_s...]
    unnamed x12 -> x6, local copies, waits for them, and re-layouts: 3.35 us -> 2.67 us
where the time goes in v2:
time: 78.4 us; the launch traced here: 78.2 us
  Pallas kernels  74.2 us (95%)
  local copies, waits for them, and re-layouts  3.3 us (4%)
    pallas_call x1, Pallas kernels, body(): pl.pallas_call(functools.partial(kernel, n, count, groups, bl, br), out_s...  74.2 us
    unnamed x6, local copies, waits for them, and re-layouts  2.67 us

profile of v2, /device:TPU:0, one launch (start us, length us, event | category | flops | bytes accessed | tf_op | source)
XLA Modules:
  0.0 78.2 jit_solution(17067698113693786169)
XLA Ops:
  0.6 74.2 %shard_map.94 = (f32[1,64,128]{2,1,0:T(8,128)}, f32[1,64,128]{2,1,0:T(8,128)}, f32[8,128]{1,0:T(8,128)}) custom-call(s32[1,512]{1,0:T(1,128)} %bitcast.5, s32[1,512]{1,0:T(1,128)} %bitcast.6, s32[1,512]{1,0:T(1,128)} %bitcast.7, f32[1,64,128]{2,1,0:T(8,128)} %psi_ref.1, f32[1,64,128]{2,1,0:T(8,128)} %pre_ref.1, bf16[32,64,64]{2,1,0:T(8,128)(2,1)} %left_ref.1, ...), custom_call_target="tpu_custom_call" | custom-call | tf_op jit(solution)/shard_map/pallas_call | solution.py:273
  74.8 0.0 copy-start.1
  74.9 0.7 copy-done.1
  75.5 0.6 slice_reduce_fusion
  76.2 0.0 copy-start
  76.2 1.4 %copy.12 = f32[1,64,128]{2,1,0:T(8,128)} copy(f32[1,64,128]{2,1,0:T(8,128)} %get-tuple-element.12) | data formatting | bytes 65536
  77.5 0.0 copy-done
  77.5 0.6 copy.13
Async XLA Ops:
  74.8 0.7 copy-start.1
  76.2 1.4 %copy-start = (f32[1,64,128]{2,1,0:T(8,128)S(1)}, f32[1,64,128]{2,1,0:T(8,128)}, u32[]{:S(2)}) copy-start(f32[1,64,128]{2,1,0:T(8,128)} %get-tuple-element.13) | copy-start | bytes 98308

commit v3 on v2

--- a/solution.py
+++ b/solution.py
@@ -114,7 +114,7 @@
         all_psi[s] = psi_recv[s].astype(F32)
         return 0
 
-    lax.fori_loop(0, n, unpack, 0)
+    lax.fori_loop(0, n, unpack, 0, unroll=4)
 
     def apply(parity, start, length, out, split):
         chunk = min(length, 8)
@@ -140,7 +140,7 @@
 
         lax.fori_loop(0, length // chunk, some, 0)
 
-    unroll = 8
+    unroll = 16
     for step in range(ITERS):
         last = step == ITERS - 1
 
@@ -193,14 +193,15 @@
         pre = pre_ref[0]
         u = psi - pre * sigma
         v = pre * psi
+        if not last:
+            u_recv[step, me] = u.astype(BF16)
+            gather(UPD + step, 1 + step, u_recv.at[step])
         rows = [jnp.sum(x, axis=0, keepdims=True) for x in (psi * psi, psi * sigma, u * u, u * v, v * v)]
         s_recv[step, me] = jnp.concatenate(rows + [jnp.zeros((3, br), F32)], axis=0)
         if last:
             sig_out[0] = sigma
             push_all(SCAL + step, s_recv.at[step])
         else:
-            u_recv[step, me] = u.astype(BF16)
-            gather(UPD + step, 1 + step, u_recv.at[step])
             push_all(SCAL + step, s_recv.at[step])
             hand_on(UPD + step, 1 + step, u_recv.at[step])
         wait_for(recv_sem, SCAL + step, s_recv.at[step, others])

time: 78.4 us -> 77.3 us (0.986)
  Pallas kernels: 74.2 us -> 73.1 us
    pallas_call x1, Pallas kernels: 74.2 us -> 73.1 us  [body(): pl.pallas_call(functools.partial(kernel, n, count, groups, bl, br), out_s...]
where the time goes in v3:
time: 77.3 us; the launch traced here: 77.1 us
  Pallas kernels  73.1 us (95%)
  local copies, waits for them, and re-layouts  3.3 us (4%)
    pallas_call x1, Pallas kernels, body(): pl.pallas_call(functools.partial(kernel, n, count, groups, bl, br), out_s...  73.1 us
    unnamed x6, local copies, waits for them, and re-layouts  2.67 us

profile of v3, /device:TPU:0, one launch (start us, length us, event | category | flops | bytes accessed | tf_op | source)
XLA Modules:
  0.0 77.1 jit_solution(9350935079768315875)
XLA Ops:
  0.6 73.1 %shard_map.94 = (f32[1,64,128]{2,1,0:T(8,128)}, f32[1,64,128]{2,1,0:T(8,128)}, f32[8,128]{1,0:T(8,128)}) custom-call(s32[1,512]{1,0:T(1,128)} %bitcast.5, s32[1,512]{1,0:T(1,128)} %bitcast.6, s32[1,512]{1,0:T(1,128)} %bitcast.7, f32[1,64,128]{2,1,0:T(8,128)} %psi_ref.1, f32[1,64,128]{2,1,0:T(8,128)} %pre_ref.1, bf16[32,64,64]{2,1,0:T(8,128)(2,1)} %left_ref.1, ...), custom_call_target="tpu_custom_call" | custom-call | tf_op jit(solution)/shard_map/pallas_call | solution.py:274
  73.8 0.0 copy-start.1
  73.8 0.7 copy-done.1
  74.5 0.6 slice_reduce_fusion
  75.1 0.0 copy-start
  75.1 1.4 %copy.12 = f32[1,64,128]{2,1,0:T(8,128)} copy(f32[1,64,128]{2,1,0:T(8,128)} %get-tuple-element.12) | data formatting | bytes 65536
  76.5 0.0 copy-done
  76.5 0.6 copy.13
Async XLA Ops:
  73.8 0.7 copy-start.1
  75.1 1.4 %copy-start = (f32[1,64,128]{2,1,0:T(8,128)S(1)}, f32[1,64,128]{2,1,0:T(8,128)}, u32[]{:S(2)}) copy-start(f32[1,64,128]{2,1,0:T(8,128)} %get-tuple-element.13) | copy-start | bytes 98308
